TPU v7x, 32 devices: a whole 2x2x4 slice. The times are simulated.
32 devices in a mesh: groups: 2 (over y), lon: 4 (over z), lat: 2 (over x), feat: 2 (over core).
Axes of the slice: x: 2, y: 2, z: 4, core: 2. Of those that a mesh axis runs over, the one named last changes fastest.
Arguments:
- pix_feat: float32 [4, 4, 64, 2048], P(('groups', 'lat'), 'lon', None, 'feat'), parts along dimension 0, may hold values from -4 to 4
- labels: int32 [4, 4, 2048], P(('groups', 'lat'), 'lon', 'feat'), parts along dimension 0, may hold values from 0 to 11
- lm_feat: float32 [4, 4, 64, 512], P(('groups', 'lat'), 'lon', None, 'feat'), parts along dimension 0, may hold values from -4 to 4
- coefs: float32 [4, 4, 12, 512], P(('groups', 'lat'), 'lon', None, 'feat'), parts along dimension 0, may hold values from -3 to 3
- direction: float32 [4, 4, 12, 512], P(('groups', 'lat'), 'lon', None, 'feat'), parts along dimension 0, may hold values from -3 to 3
- pair_pix: int32 [4, 4, 512], P(('groups', 'lat'), 'lon', 'feat'), parts along dimension 0, may hold values from 0 to 7
- pair_lm: int32 [4, 4, 512], P(('groups', 'lat'), 'lon', 'feat'), parts along dimension 0, may hold values from 0 to 35, as said below
- pair_count: int32 [4, 4, 2], P(('groups', 'lat'), 'lon', 'feat'), parts along dimension 0, may hold values from 4 to 256, as said below
Outputs:
- gradient: float32 [4, 4, 12, 512], P(('groups', 'lat'), 'lon', None, 'feat'), parts along dimension 0
- hess_vec: float32 [4, 4, 12, 512], P(('groups', 'lat'), 'lon', None, 'feat'), parts along dimension 0
There are 2 independent parts, one for each index of `groups`. A program takes and returns all parts, laid end to end along the dimension named above; each array names one. Nothing has to cross between parts.
Inputs may be any that keep to these rules, and one draw needn't show every extreme that they name: `pair_count`: slots at or past their half tile's count hold valid entries that are ignored. `pair_lm`: no block of band 0 names a neighbour in band -1 and no block of band 2 - 1 one in band 2.
All inputs are finite; a program needn't handle non-finite values.
Results may differ from a plain program's by a relative error of at most 0.0003.
Values sent between devices are 32-bit elements; how exact they have to be, the bound alone decides.
A program may use at most 64 MiB of HBM per device.

v0:
```python
import jax
import jax.numpy as jnp
from jax import lax
from jax.sharding import PartitionSpec as P

FEATS = 64
CLASSES = 12
BLOCK = 128


kernel_radius = 5.0


def from_behind(value, axis, steps):
    count = lax.axis_size(axis)
    leading, last = (max(0, -steps), min(count, count - steps))
    return lax.ppermute(value, axis, [(source, source + steps) for source in range(leading, last)])


def from_behind_2(shard, axis, by):
    devices = lax.axis_size(axis)
    return lax.ppermute(shard, axis, [(i, (i + by) % devices) for i in range(devices)])


def padded(cells, sides, width):
    for axis, dim in sides:
        count = lax.axis_size(axis)
        head = lax.slice_in_dim(cells, 0, width, axis=dim)
        tail = lax.slice_in_dim(cells, cells.shape[dim] - width, cells.shape[dim], axis=dim)
        cells = jnp.concatenate(
            [
                lax.ppermute(tail, axis, [(i, (i + 1) % count) for i in range(count)]),
                cells,
                lax.ppermute(head, axis, [((i + 1) % count, i) for i in range(count)]),
            ],
            axis=dim,
        )
    return cells


def lat_back_whole(values, offset):
    return from_behind(values, "lat", offset)


def lon_back_whole(values, offset):
    return from_behind_2(values, "lon", offset)


def body(pix_feat, labels, lm_feat, coefs, direction, pair_pix, pair_lm, pair_count):
    own_data = jnp.concatenate([lm_feat, coefs, direction], axis=2)
    whole_tile = lax.all_gather(own_data, "feat", axis=3, tiled=True)
    near = padded(whole_tile, (("lon", 1), ("lat", 0)), 1)
    tile_width = near.shape[3]
    lm_blocks_tile = tile_width // BLOCK
    near_count = 9 * lm_blocks_tile
    rows_data = FEATS + 2 * CLASSES
    stacked = near.reshape(3, 3, rows_data, lm_blocks_tile, BLOCK)
    stacked = stacked.transpose(0, 1, 3, 2, 4).reshape(near_count, rows_data, BLOCK)
    lm_blocks = stacked[:, :FEATS]
    coefficient_tiles = stacked[:, FEATS:]
    lm_sq = jnp.sum(lm_blocks * lm_blocks, axis=1)
    pixels = pix_feat[0, 0]
    pix_count = pixels.shape[1] // BLOCK
    pix_blocks = pixels.reshape(FEATS, pix_count, BLOCK).transpose(1, 0, 2)
    pix_sq = jnp.sum(pix_blocks * pix_blocks, axis=1)
    slots_pix = pair_pix[0, 0]
    slots_lm = pair_lm[0, 0]
    count = pair_count[0, 0, 0]
    slot_total = slots_pix.shape[0]
    group = min(16, slot_total)
    turns = (count + group - 1) // group
    pix_iota = jnp.arange(pix_count, dtype=jnp.int32)
    near_iota = jnp.arange(near_count, dtype=jnp.int32)

    def group_slots(turn_index):
        start = turn_index * group
        slot_pixel = lax.dynamic_slice_in_dim(slots_pix, start, group)
        slot_landmark = lax.dynamic_slice_in_dim(slots_lm, start, group)
        live_mask = (start + jnp.arange(group, dtype=jnp.int32) < count).astype(jnp.float32)
        return (slot_pixel, slot_landmark, live_mask)

    def kernel_block(slot_pixel, slot_landmark, live_mask):
        pix_rows = pix_blocks[slot_pixel]
        lm_rows = lm_blocks[slot_landmark]
        cross = jnp.einsum("gfp,gfl->gpl", pix_rows, lm_rows, precision=lax.Precision.HIGHEST)
        distance = pix_sq[slot_pixel][:, :, None] + lm_sq[slot_landmark][:, None, :] - 2.0 * cross
        scaled = jnp.sqrt(distance) / kernel_radius
        remain = jnp.maximum(1.0 - scaled, 0.0)
        squared = remain * remain
        return squared * squared * (4.0 * scaled + 1.0) * live_mask[:, None, None]

    saved_init = jnp.zeros((slot_total, BLOCK, BLOCK), jnp.float32)
    forward_init = jnp.zeros((pix_count, 2 * CLASSES, BLOCK), jnp.float32)

    def forward_step(turn_index, carry):
        forward, saved = carry
        slot_pixel, slot_landmark, live_mask = group_slots(turn_index)
        kernel_weight = kernel_block(slot_pixel, slot_landmark, live_mask)
        contribution = jnp.einsum(
            "vjz,vhz->vjh",
            coefficient_tiles[slot_landmark],
            kernel_weight,
            precision=lax.Precision.HIGHEST,
        )
        selector_matrix = (slot_pixel[:, None] == pix_iota[None, :]).astype(
            jnp.float32
        ) * live_mask[:, None]
        forward = forward + jnp.einsum(
            "ha,hro->aro", selector_matrix, contribution, precision=lax.Precision.HIGHEST
        )
        saved = lax.dynamic_update_slice_in_dim(saved, kernel_weight, turn_index * group, 0)
        return (forward, saved)

    forward, saved = lax.fori_loop(0, turns, forward_step, (forward_init, saved_init))
    logits = forward[:, :CLASSES]
    probe = forward[:, CLASSES:]
    highest = jnp.max(logits, axis=1, keepdims=True)
    powered = jnp.exp(logits - highest)
    chances = powered / jnp.sum(powered, axis=1, keepdims=True)
    label_blocks = labels[0, 0].reshape(pix_count, BLOCK)
    target = (
        label_blocks[:, None, :] == jnp.arange(CLASSES, dtype=jnp.int32)[None, :, None]
    ).astype(jnp.float32)
    resid = chances - target
    curv = chances * probe - chances * jnp.sum(chances * probe, axis=1, keepdims=True)
    reverse_sweep = jnp.concatenate([resid, curv], axis=1)

    def backward_step(turn_index, landed):
        slot_pixel, slot_landmark, live_mask = group_slots(turn_index)
        kernel_weight = lax.dynamic_slice_in_dim(saved, turn_index * group, group, 0)
        partial_pieces = jnp.einsum(
            "sjr,sru->sju",
            reverse_sweep[slot_pixel],
            kernel_weight,
            precision=lax.Precision.HIGHEST,
        )
        selector_matrix = (slot_landmark[:, None] == near_iota[None, :]).astype(
            jnp.float32
        ) * live_mask[:, None]
        return landed + jnp.einsum(
            "gn,gcl->ncl", selector_matrix, partial_pieces, precision=lax.Precision.HIGHEST
        )

    landed = lax.fori_loop(
        0, turns, backward_step, jnp.zeros((near_count, 2 * CLASSES, BLOCK), jnp.float32)
    )
    landed = landed.reshape(3, 3, lm_blocks_tile, 2 * CLASSES, BLOCK).transpose(0, 1, 3, 2, 4)
    partial_sums = landed.reshape(3, 3, 2 * CLASSES, tile_width)
    lat_done = (
        partial_sums[1] + lat_back_whole(partial_sums[0], -1) + lat_back_whole(partial_sums[2], 1)
    )
    lon_done = lat_done[1] + lon_back_whole(lat_done[0], -1) + lon_back_whole(lat_done[2], 1)
    owned = lax.psum_scatter(lon_done, "feat", scatter_dimension=1, tiled=True)
    gradient = owned[:CLASSES][None, None]
    hess_vec = owned[CLASSES:][None, None]
    return (gradient, hess_vec)


def solution(mesh):
    placed = (
        P(("groups", "lat"), "lon", None, "feat"),
        P(("groups", "lat"), "lon", "feat"),
        P(("groups", "lat"), "lon", None, "feat"),
        P(("groups", "lat"), "lon", None, "feat"),
        P(("groups", "lat"), "lon", None, "feat"),
        P(("groups", "lat"), "lon", "feat"),
        P(("groups", "lat"), "lon", "feat"),
        P(("groups", "lat"), "lon", "feat"),
    )
    return jax.shard_map(
        body,
        mesh=mesh,
        in_specs=placed,
        out_specs=(
            P(("groups", "lat"), "lon", None, "feat"),
            P(("groups", "lat"), "lon", None, "feat"),
        ),
        check_vma=False,
    )
```

profile of v0, /device:TPU:0, one launch (start us, length us, event | category | flops | bytes accessed | tf_op | source)
XLA Modules:
  0.0 378.0 jit_solution(17015905026329400922)
XLA Ops:
  9.5 2.0 all_gather.3
  11.6 2.9 collective-permute-start
  14.5 2.0 collective-permute-start.1
  16.5 5.4 %collective-permute-done = f32[1,1,88,512]{3,2,1,0:T(8,128)S(1)} collective-permute-done((f32[1,1,88,512]{3,2,1,0:T(8,128)S(1)}, f32[1,1,88,512]{3,2,1,0:T(8,128)S(1)}, u32[]{:S(2)}, u32[]{:S(2)}) %collective-permute-start) | collective-permute-done | bytes 180256 | tf_op jit(solution)/shard_map/ppermute | solution.py:32
  21.9 2.7 collective-permute-done.1
  24.7 1.6 collective-permute-start.2
  27.7 12.3 %collective-permute-done.2 = f32[1,3,88,512]{3,2,1,0:T(8,128)S(1)} collective-permute-done((f32[1,3,88,512]{3,2,1,0:T(8,128)S(1)}, f32[1,3,88,512]{3,2,1,0:T(8,128)S(1)}, u32[]{:S(2)}, u32[]{:S(2)}) %collective-permute-start.2) | collective-permute-done | bytes 540704 | tf_op jit(solution)/shard_map/ppermute | solution.py:32
  40.0 10.0 %collective-permute-done.3 = f32[1,3,88,512]{3,2,1,0:T(8,128)S(1)} collective-permute-done((f32[1,3,88,512]{3,2,1,0:T(8,128)S(1)}, f32[1,3,88,512]{3,2,1,0:T(8,128)S(1)}, u32[]{:S(2)}, u32[]{:S(2)}) %collective-permute-start.3) | collective-permute-done | bytes 540704 | tf_op jit(solution)/shard_map/ppermute | solution.py:34
  51.1 7.9 %broadcast_in_dim.48 = f32[256,128,128]{2,1,0:T(8,128)} broadcast(f32[]{:T(128)} %constant.95.clone.1), dimensions={} | broadcast | bytes 16777220 | tf_op jit(solution)/shard_map/broadcast_in_dim | solution.py:92
  59.7 13.5 %while.26 = (s32[]{:T(128)}, f32[8,24,128]{2,0,1:T(8,128)}, f32[256,128,128]{2,1,0:T(8,128)}, s32[]{:T(128)}, s32[256]{0:T(256)S(1)}, /*index=5*/s32[]{:T(128)},...) while((s32[]{:T(128)}, f32[8,24,128]{2,0,1:T(8,128)}, ...), condition=%wide.region_3.4_spmd.clone, body=%wide.region_2.3_spmd.clone.sunk | while | flops 284715392 | bytes 7686311 | solution.py:114
  62.1 1.2 gather_fusion.4
  63.9 4.1 %constant_dynamic-update-slice_fusion.5 = (f32[256,128,128]{2,1,0:T(8,128)}, f32[16,128,128]{2,1,0:T(8,128)S(1)}) fusion(f32[256,128,128]{2,1,0:T(8,128)} %get-tuple-element.498, s32[]{:T(128)S(6)} %select_n.50, f32[16]{0:T(128)S(1)} %compare_convert_fusion.4, f32[16,64,128]{2,1,0:T(8,128)S(1)} %gather_fusion.1, ...), kind=kOutput, calls=%fused_computation.25.clone.1 | convolution fusion | flops 204472320 | bytes 3162180 | tf_op jit(solution)/shard_map/while/body/gfp,gfl->gpl/dot_general | solution.py:85
  68.0 1.6 gather_fusion
  69.6 1.7 fusion.64
  71.4 1.8 convolution_add_fusion.4
  75.1 4.4 %while.27 = (s32[]{:T(128)}, f32[36,24,128]{2,0,1:T(8,128)S(1)}, s32[]{:T(128)}, s32[256]{0:T(256)S(1)}, s32[]{:T(128)}, /*index=5*/s32[256]{0:T(256)S(1)}, f32[...) while((s32[]{:T(128)}, f32[36,24,128]{2,0,1:T(8,128)S(1)}, ...), condition=%wide.region_8.9_spmd.clone, body=%wide.region_7.8_spmd.clone.sunk | while | flops 96844008 | bytes 2921207 | solution.py:144
  75.8 2.2 fusion.69
  79.7 1.3 collective-permute-start.4
  81.1 4.6 %collective-permute-start.5 = (f32[3,24,512]{2,1,0:T(8,128)S(1)}, f32[3,24,512]{2,1,0:T(8,128)S(1)}, u32[]{:S(2)}, u32[]{:S(2)}) collective-permute-start(f32[3,24,512]{2,1,0:T(8,128)S(1)} %squeeze.32), channel_id=1, source_target_pairs={{0,2},{1,3},{4,6},{5,7},{8,10},{9,11},{12,14},{13,15},{16,18},{17,... | collective-permute-start | bytes 442376 | tf_op jit(solution)/shard_map/ppermute | solution.py:17
  86.7 1.6 collective-permute-done.5
  88.4 55.7 %collective-permute-start.6 = (f32[24,512]{1,0:T(8,128)S(1)}, f32[24,512]{1,0:T(8,128)S(1)}, u32[]{:S(2)}, u32[]{:S(2)}) collective-permute-start(f32[24,512]{1,0:T(8,128)S(1)} %get-tuple-element.340), channel_id=1, source_target_pairs={{0,12},{4,0},{8,4},{12,8},{1,13},{5,1},{9,5},{13,9},{2,14},{6,2},{... | collective-permute-start | bytes 147464 | tf_op jit(solution)/shard_map/ppermute | solution.py:22
  144.1 1.7 collective-permute-done.6
  145.8 215.4 %collective-permute-done.7 = f32[24,512]{1,0:T(8,128)S(1)} collective-permute-done((f32[24,512]{1,0:T(8,128)S(1)}, f32[24,512]{1,0:T(8,128)S(1)}, u32[]{:S(2)}, u32[]{:S(2)}) %collective-permute-start.7) | collective-permute-done | bytes 49184 | tf_op jit(solution)/shard_map/ppermute | solution.py:22
  361.9 7.2 %reduce-scatter.2.cloned.1.call-done = f32[24,256]{1,0:T(8,128)} async-done(((f32[24,512]{1,0:T(8,128)}), f32[24,256]{1,0:T(8,128)}) %reduce-scatter.2.cloned.1.call-update) | async-done | bytes 24592 | tf_op jit(solution)/shard_map/reduce_scatter | solution.py:153
  (70 shorter events, 16.0 us)
Async XLA Ops:
  7.2 20.3 %copy-start.2 = (f32[1,1,64,1024]{3,2,1,0:T(8,128)S(1)}, f32[1,1,64,1024]{3,2,1,0:T(8,128)}, u32[]{:S(2)}) copy-start(f32[1,1,64,1024]{3,2,1,0:T(8,128)} %param.12) | copy-start | bytes 786436
  7.2 362.0 %reduce-scatter.2.cloned.1.call-start = ((), (), s32[]{:S(2)}) async-start(), calls=%async_computation.1 | async-start | bytes 73728 | tf_op jit(solution)/shard_map/reduce_scatter | solution.py:153
  11.6 10.3 %collective-permute-start = (f32[1,1,88,512]{3,2,1,0:T(8,128)S(1)}, f32[1,1,88,512]{3,2,1,0:T(8,128)S(1)}, u32[]{:S(2)}, u32[]{:S(2)}) collective-permute-start(f32[1,1,88,512]{3,2,1,0:T(8,128)S(1)} %all_gather.3), channel_id=1, source_target_pairs={{0,4},{4,8},{8,12},{12,0},{1,5},{5,9},{9,13},{13,1},{2,6},{6,10},{... | collective-permute-start | bytes 540680 | tf_op jit(solution)/shard_map/ppermute | solution.py:32
  14.5 10.2 %collective-permute-start.1 = (f32[1,1,88,512]{3,2,1,0:T(8,128)S(1)}, f32[1,1,88,512]{3,2,1,0:T(8,128)S(1)}, u32[]{:S(2)}, u32[]{:S(2)}) collective-permute-start(f32[1,1,88,512]{3,2,1,0:T(8,128)S(1)} %all_gather.3), channel_id=1, source_target_pairs={{4,0},{8,4},{12,8},{0,12},{5,1},{9,5},{13,9},{1,13},{6,2},{10,6},{... | collective-permute-start | bytes 540680 | tf_op jit(solution)/shard_map/ppermute | solution.py:34
  24.7 15.3 %collective-permute-start.2 = (f32[1,3,88,512]{3,2,1,0:T(8,128)S(1)}, f32[1,3,88,512]{3,2,1,0:T(8,128)S(1)}, u32[]{:S(2)}, u32[]{:S(2)}) collective-permute-start(f32[1,3,88,512]{3,2,1,0:T(8,128)S(1)} %constant_dynamic-update-slice_fusion.1), channel_id=1, source_target_pairs={{0,2},{2,0},{1,3},{3,1},{4,6},{6,4},{5,7},{7,5},{8,10},{10,8},{9,1... | collective-permute-start | bytes 1622024 | tf_op jit(solution)/shard_map/ppermute | solution.py:32
  26.2 23.7 %collective-permute-start.3 = (f32[1,3,88,512]{3,2,1,0:T(8,128)S(1)}, f32[1,3,88,512]{3,2,1,0:T(8,128)S(1)}, u32[]{:S(2)}, u32[]{:S(2)}) collective-permute-start(f32[1,3,88,512]{3,2,1,0:T(8,128)S(1)} %constant_dynamic-update-slice_fusion.1), channel_id=1, source_target_pairs={{2,0},{0,2},{3,1},{1,3},{6,4},{4,6},{7,5},{5,7},{10,8},{8,10},{11,... | collective-permute-start | bytes 1622024 | tf_op jit(solution)/shard_map/ppermute | solution.py:34
  51.1 8.5 %copy-start.6 = (s32[1,1,256]{2,1,0:T(1,128)S(1)}, s32[1,1,256]{2,1,0:T(1,128)}, u32[]{:S(2)}) copy-start(s32[1,1,256]{2,1,0:T(1,128)} %param.18) | copy-start | bytes 3076
  51.1 8.5 %copy-start.8 = (s32[1,1,256]{2,1,0:T(1,128)S(1)}, s32[1,1,256]{2,1,0:T(1,128)}, u32[]{:S(2)}) copy-start(s32[1,1,256]{2,1,0:T(1,128)} %param.17) | copy-start | bytes 3076
  59.7 1.8 copy-start
  63.9 4.1 %copy-start.4 = (f32[16]{0:T(128)}, f32[16]{0:T(128)S(1)}, u32[]{:S(2)}) copy-start(f32[16]{0:T(128)S(1)} %compare_convert_fusion.4) | copy-start | bytes 196 | tf_op jit(solution)/shard_map/while
  68.0 3.4 copy-start.3
  68.0 5.2 %copy-start.1 = (f32[36,128]{1,0:T(8,128)S(1)}, f32[36,128]{1,0:T(8,128)}, u32[]{:S(2)}) copy-start(f32[36,128]{1,0:T(8,128)} %copy-done) | copy-start | bytes 55300 | tf_op jit(solution)/shard_map/while
  68.0 5.2 %copy-start.7 = (s32[1,1,256]{2,1,0:T(1,128)S(1)}, s32[1,1,256]{2,1,0:T(1,128)}, u32[]{:S(2)}) copy-start(s32[1,1,256]{2,1,0:T(1,128)} %get-tuple-element.600) | copy-start | bytes 3076 | tf_op jit(solution)/shard_map/while
  68.0 5.2 %copy-start.9 = (s32[1,1,256]{2,1,0:T(1,128)S(1)}, s32[1,1,256]{2,1,0:T(1,128)}, u32[]{:S(2)}) copy-start(s32[1,1,256]{2,1,0:T(1,128)} %get-tuple-element.618) | copy-start | bytes 3076 | tf_op jit(solution)/shard_map/while
  68.0 3.4 copy-start.5
  79.7 7.0 %collective-permute-start.4 = (f32[3,24,512]{2,1,0:T(8,128)S(1)}, f32[3,24,512]{2,1,0:T(8,128)S(1)}, u32[]{:S(2)}, u32[]{:S(2)}) collective-permute-start(f32[3,24,512]{2,1,0:T(8,128)S(1)} %squeeze.31), channel_id=1, source_target_pairs={{2,0},{3,1},{6,4},{7,5},{10,8},{11,9},{14,12},{15,13},{18,16},{19,... | collective-permute-start | bytes 442376 | tf_op jit(solution)/shard_map/ppermute | solution.py:17
  81.1 7.2 %collective-permute-start.5 = (f32[3,24,512]{2,1,0:T(8,128)S(1)}, f32[3,24,512]{2,1,0:T(8,128)S(1)}, u32[]{:S(2)}, u32[]{:S(2)}) collective-permute-start(f32[3,24,512]{2,1,0:T(8,128)S(1)} %squeeze.32), channel_id=1, source_target_pairs={{0,2},{1,3},{4,6},{5,7},{8,10},{9,11},{12,14},{13,15},{16,18},{17,... | collective-permute-start | bytes 442376 | tf_op jit(solution)/shard_map/ppermute | solution.py:17
  88.4 57.5 %collective-permute-start.6 = (f32[24,512]{1,0:T(8,128)S(1)}, f32[24,512]{1,0:T(8,128)S(1)}, u32[]{:S(2)}, u32[]{:S(2)}) collective-permute-start(f32[24,512]{1,0:T(8,128)S(1)} %get-tuple-element.340), channel_id=1, source_target_pairs={{0,12},{4,0},{8,4},{12,8},{1,13},{5,1},{9,5},{13,9},{2,14},{6,2},{... | collective-permute-start | bytes 147464 | tf_op jit(solution)/shard_map/ppermute | solution.py:22
  144.1 217.2 %collective-permute-start.7 = (f32[24,512]{1,0:T(8,128)S(1)}, f32[24,512]{1,0:T(8,128)S(1)}, u32[]{:S(2)}, u32[]{:S(2)}) collective-permute-start(f32[24,512]{1,0:T(8,128)S(1)} %get-tuple-element.341), channel_id=1, source_target_pairs={{0,4},{4,8},{8,12},{12,0},{1,5},{5,9},{9,13},{13,1},{2,6},{6,10},{... | collective-permute-start | bytes 147464 | tf_op jit(solution)/shard_map/ppermute | solution.py:22
Sparse Core Ops, SparseCore 0:
  362.1 7.0 reduce-scatter.1
where the time goes:
time: 382 us; the launch traced here: 378 us
  waiting for transfers between devices  257 us (67%)
  starting transfers between devices  68.7 us (18%)
  local copies, waits for them, and re-layouts  19.5 us (5%)
  between operations  14.9 us (4%)
  matrix products  10.5 us (3%)
  other arithmetic  4.93 us (1%)
    ppermute x2, waiting for transfers between devices, from_behind_2(): lax.ppermute(shard, axis, [(i, (i + by) % devices) for i in range(devices)])  217 us
    ppermute x2, starting transfers between devices, from_behind_2(): lax.ppermute(shard, axis, [(i, (i + by) % devices) for i in range(devices)])  55.7 us
    ppermute x2, waiting for transfers between devices, padded(): lax.ppermute(tail, axis, [(i, (i + 1) % count) for i in range(count)])  17.7 us
    ppermute x2, waiting for transfers between devices, padded(): lax.ppermute(head, axis, [((i + 1) % count, i) for i in range(count)])  12.7 us
    broadcast_in_dim x1, local copies, waits for them, and re-layouts, body(): saved_init = jnp.zeros((slot_total, BLOCK, BLOCK), jnp.float32)  7.87 us
  transfers between devices with their start and end apart: 9, of which 9 were waited for; matrix products, arithmetic and copies ran while one was open for 0% of the time, Pallas kernels for 0%

commit v1 on v0

v1 whole, which is shorter than its diff:
```python
import functools

import jax
import jax.numpy as jnp
from jax import lax
from jax.experimental import pallas as pl
from jax.experimental.pallas import tpu as pltpu
from jax.sharding import PartitionSpec as P

BLOCK = 128
CHUNK = 256
RADIUS = 5.0
BF16 = jnp.bfloat16
F32 = jnp.float32
NN = (((1,), (0,)), ((), ()))
NT = (((1,), (1,)), ((), ()))


def dot(left, right, numbers):
    return lax.dot_general(left, right, numbers, preferred_element_type=F32)


def parts_of(value):
    high = value.astype(BF16).astype(F32)
    return high, value - high


def three_parts(value):
    first, rest = parts_of(value)
    second, third = parts_of(rest)
    return first, second, third


def stacked_pair(value, rows):
    high, low = parts_of(value)
    both = jnp.concatenate([high, low], axis=0).astype(BF16)
    pad = jnp.zeros((rows - value.shape[0], value.shape[1]), F32)
    return both, jnp.concatenate([high, pad], axis=0).astype(BF16)


def kernel(
    lats,
    lons,
    lm_ref,
    co_ref,
    di_ref,
    px_ref,
    lab_ref,
    pp_ref,
    pn_ref,
    cnt_ref,
    grad_ref,
    hess_ref,
    near,
    kern_hi,
    kern_lo,
    pix_rows,
    weight,
    forward,
    back_both,
    back_high,
    mine,
    part_out,
    part_in,
    tot_out,
    tot_in,
    near_send,
    near_recv,
    pass_send,
    part_send,
    part_recv,
    tot_send,
    tot_recv,
):
    feats, half_lm = lm_ref.shape[2:]
    classes = co_ref.shape[2]
    rows = 2 * classes
    pix = px_ref.shape[3]
    depth = pix_rows.shape[1]
    slots = pp_ref.shape[2]
    side = lax.axis_index("feat")
    band = lax.axis_index("lat")
    column = lax.axis_index("lon")
    partner = {"feat": 1 - side}

    def inside(a):
        return jnp.logical_and(band + a >= 1, band + a <= lats)

    def tile_at(a, b):
        return {"lat": band + a - 1, "lon": lax.rem(column + b - 1 + lons, lons)}

    def order(turn):
        return lax.rem(1 + 2 * lax.rem(turn, 3), 3), lax.rem(1 + 2 * (turn // 3), 3)

    around = [(1, 0), (1, 2), (0, 0), (0, 2), (2, 0), (2, 2), (0, 1), (2, 1)]

    def each_around(act):
        for a, b in around:
            if a == 1:
                act(a, b)
            else:
                pl.when(inside(a))(functools.partial(act, a, b))

    barrier = pltpu.get_barrier_semaphore()

    def greet(a, b):
        pl.semaphore_signal(barrier, inc=1, device_id=tile_at(a, b), device_id_type=pl.DeviceIdType.MESH)

    pl.semaphore_signal(barrier, inc=1, device_id=partner, device_id_type=pl.DeviceIdType.MESH)
    each_around(greet)

    own = 8 + side
    near[own, 0:feats, :] = lm_ref[0, 0]
    near[own, feats : feats + classes, :] = co_ref[0, 0]
    near[own, feats + classes : feats + rows, :] = di_ref[0, 0]

    bands = sum(inside(a).astype(jnp.int32) for a in (0, 1, 2))
    pl.semaphore_wait(barrier, 3 * bands)

    def near_copy(a, b):
        there = (2 - a) * 3 + (2 - b)
        return pltpu.make_async_remote_copy(
            src_ref=near.at[own],
            dst_ref=near.at[2 * there + side],
            send_sem=near_send.at[a * 3 + b],
            recv_sem=near_recv.at[2 * there + side],
            device_id=tile_at(a, b),
            device_id_type=pl.DeviceIdType.MESH,
        )

    def pass_copy(slot):
        return pltpu.make_async_remote_copy(
            src_ref=near.at[2 * slot + side],
            dst_ref=near.at[2 * slot + side],
            send_sem=pass_send.at[slot],
            recv_sem=near_recv.at[2 * slot + side],
            device_id=partner,
            device_id_type=pl.DeviceIdType.MESH,
        )

    def arrived(place):
        return pltpu.make_async_remote_copy(
            src_ref=near.at[place],
            dst_ref=near.at[place],
            send_sem=near_send.at[4],
            recv_sem=near_recv.at[place],
            device_id=partner,
            device_id_type=pl.DeviceIdType.MESH,
        )

    pass_copy(4).start()
    each_around(lambda a, b: near_copy(a, b).start())

    pixels = px_ref[0, 0]
    x_high, x_low = parts_of(pixels * (-2.0 / (RADIUS * RADIUS)))
    x1, x2, x3 = three_parts(jnp.sum(pixels * pixels, axis=0, keepdims=True) * (1.0 / (RADIUS * RADIUS)))
    row = lax.broadcasted_iota(jnp.int32, (depth - 3 * feats, pix), 0)
    extra = jnp.where(
        row < 3,
        1.0,
        jnp.where(row == 3, x1, jnp.where(row == 4, x2, jnp.where(row == 5, x3, 0.0))),
    )
    pix_rows[...] = jnp.concatenate([x_high, x_high, x_low, extra], axis=0).T.astype(BF16)

    pix_blocks = pix // BLOCK
    near_blocks = 18 * half_lm // BLOCK
    used = lax.broadcasted_iota(jnp.int32, (1, slots), 1) < cnt_ref[0, 0, 0]
    pix_hot = jnp.where(
        jnp.logical_and(lax.broadcasted_iota(jnp.int32, (pix_blocks, slots), 0) == pp_ref[0], used), 1.0, 0.0
    ).astype(BF16)
    lm_pad = -(-near_blocks // BLOCK) * BLOCK
    lm_hot = jnp.where(lax.broadcasted_iota(jnp.int32, (lm_pad, slots), 0) == pn_ref[0], 1.0, 0.0).astype(BF16)
    counts = dot(pix_hot, lm_hot, NT).astype(BF16)
    width = near_blocks * BLOCK
    spread = jnp.where(
        lax.broadcasted_iota(jnp.int32, (lm_pad, width), 0)
        == lax.broadcasted_iota(jnp.int32, (lm_pad, width), 1) // BLOCK,
        1.0,
        0.0,
    ).astype(BF16)
    wide = dot(counts, spread, NN)
    for place in range(18):
        weight[place] = wide[:, place * half_lm : (place + 1) * half_lm]

    forward[...] = jnp.zeros_like(forward)
    aux_row = lax.broadcasted_iota(jnp.int32, (depth - 3 * feats, half_lm), 0)

    def forward_half(place):
        z = near[place, 0:feats, :]
        z_high, z_low = parts_of(z)
        z1, z2, z3 = three_parts(jnp.sum(z * z, axis=0, keepdims=True) * (1.0 / (RADIUS * RADIUS)))
        extra = jnp.where(
            aux_row == 0,
            z1,
            jnp.where(aux_row == 1, z2, jnp.where(aux_row == 2, z3, jnp.where(aux_row < 6, 1.0, 0.0))),
        )
        columns = jnp.concatenate([z_high, z_low, z_high, extra], axis=0).astype(BF16)
        both, high = stacked_pair(near[place, feats : feats + rows, :], 32)
        for chunk in range(pix // CHUNK):
            at = slice(chunk * CHUNK, (chunk + 1) * CHUNK)
            dist = jnp.maximum(dot(pix_rows[at, :], columns, NN), 1e-30)
            remain = jnp.maximum(1.0 - dist * lax.rsqrt(dist), 0.0)
            first = chunk * (CHUNK // BLOCK)
            times = jnp.concatenate(
                [
                    jnp.broadcast_to(weight[place, q : q + 1, :], (BLOCK, half_lm))
                    for q in range(first, first + CHUNK // BLOCK)
                ],
                axis=0,
            )
            squared = remain * remain
            value = squared * squared * (5.0 * times - (4.0 * times) * remain)
            value_high = value.astype(BF16)
            value_low = (value - value_high.astype(F32)).astype(BF16)
            kern_hi[place, at, :] = value_high
            kern_lo[place, at, :] = value_low
            upper = dot(both, value_high, NT)
            lower = dot(high, value_low, NT)
            forward[:, at] += upper[:rows] + upper[rows:] + lower[:rows]

    def forward_tile(turn, carry):
        a, b = order(turn)
        slot = a * 3 + b

        @pl.when(inside(a))
        def _():
            @pl.when(turn > 0)
            def _():
                arrived(2 * slot + side).wait_recv()
                pass_copy(slot).start()

            forward_half(2 * slot + side)
            arrived(2 * slot + 1 - side).wait_recv()
            forward_half(2 * slot + 1 - side)

        return carry

    lax.fori_loop(0, 9, forward_tile, 0)

    logits = forward[0:classes, :]
    probe = forward[classes:rows, :]
    powered = jnp.exp(logits - jnp.max(logits, axis=0, keepdims=True))
    chances = powered / jnp.sum(powered, axis=0, keepdims=True)
    target = jnp.where(lax.broadcasted_iota(jnp.int32, (classes, pix), 0) == lab_ref[0], 1.0, 0.0)
    moved = chances * probe
    curv = moved - chances * jnp.sum(moved, axis=0, keepdims=True)
    both, high = stacked_pair(jnp.concatenate([chances - target, curv], axis=0), 32)
    back_both[...] = both
    back_high[...] = high

    def part_copy(slot):
        return pltpu.make_async_remote_copy(
            src_ref=part_out.at[slot],
            dst_ref=part_in.at[slot],
            send_sem=part_send.at[slot],
            recv_sem=part_recv.at[slot],
            device_id=partner,
            device_id_type=pl.DeviceIdType.MESH,
        )

    def tot_copy(a, b):
        slot = a * 3 + b
        return pltpu.make_async_remote_copy(
            src_ref=tot_out.at[slot],
            dst_ref=tot_in.at[8 - slot],
            send_sem=tot_send.at[slot],
            recv_sem=tot_recv.at[8 - slot],
            device_id=tile_at(a, b),
            device_id_type=pl.DeviceIdType.MESH,
        )

    def backward_half(place):
        upper = dot(back_both[...], kern_hi[place], NN)
        lower = dot(back_high[...], kern_lo[place], NN)
        return upper[:rows] + upper[rows:] + lower[:rows]

    def backward_tile(turn, carry):
        a, b = order(8 - turn)
        slot = a * 3 + b

        @pl.when(inside(a))
        def _():
            part_out[slot] = backward_half(2 * slot + 1 - side)
            part_copy(slot).start()
            mine[slot] = backward_half(2 * slot + side)

        a_before, b_before = order(9 - turn)
        before = a_before * 3 + b_before

        @pl.when(jnp.logical_and(turn > 0, inside(a_before)))
        def _():
            part_copy(before).wait_recv()
            tot_out[before] = mine[before] + part_in[before]
            tot_copy(a_before, b_before).start()

        return carry

    lax.fori_loop(0, 9, backward_tile, 0)
    part_copy(4).wait_recv()
    tot_out[4] = mine[4] + part_in[4]

    def take(a, b):
        slot = a * 3 + b
        tot_copy(2 - a, 2 - b).wait_recv()
        tot_out[4] += tot_in[slot]

    each_around(take)
    total = tot_out[4]
    grad_ref[0, 0] = total[:classes]
    hess_ref[0, 0] = total[classes:]

    pass_copy(4).wait_send()
    part_copy(4).wait_send()

    def drain(a, b):
        near_copy(a, b).wait_send()
        pass_copy(a * 3 + b).wait_send()
        part_copy(a * 3 + b).wait_send()
        tot_copy(a, b).wait_send()

    each_around(drain)


def solution(mesh):
    lats, lons = mesh.shape["lat"], mesh.shape["lon"]

    def body(pix_feat, labels, lm_feat, coefs, direction, pair_pix, pair_lm, pair_count):
        feats, half_lm = lm_feat.shape[2:]
        rows = 2 * coefs.shape[2]
        pix = pix_feat.shape[3]
        depth = 4 * feats
        vmem = pl.BlockSpec(memory_space=pltpu.VMEM)
        out = jax.ShapeDtypeStruct(coefs.shape, F32)
        partial = pltpu.VMEM((9, rows, half_lm), F32)
        nine = pltpu.SemaphoreType.DMA((9,))
        return pl.pallas_call(
            functools.partial(kernel, lats, lons),
            out_shape=(out, out),
            in_specs=[vmem] * 7 + [pl.BlockSpec(memory_space=pltpu.SMEM)],
            out_specs=(vmem, vmem),
            scratch_shapes=[
                pltpu.VMEM((18, feats + rows, half_lm), F32),
                pltpu.VMEM((18, pix, half_lm), BF16),
                pltpu.VMEM((18, pix, half_lm), BF16),
                pltpu.VMEM((pix, depth), BF16),
                pltpu.VMEM((18, pix // BLOCK, half_lm), F32),
                pltpu.VMEM((rows, pix), F32),
                pltpu.VMEM((2 * rows, pix), BF16),
                pltpu.VMEM((32, pix), BF16),
                partial,
                partial,
                partial,
                partial,
                partial,
                nine,
                pltpu.SemaphoreType.DMA((18,)),
                nine,
                nine,
                nine,
                nine,
                nine,
            ],
            compiler_params=pltpu.CompilerParams(
                collective_id=0, has_side_effects=True, vmem_limit_bytes=48 * 1024 * 1024
            ),
        )(lm_feat, coefs, direction, pix_feat, labels, pair_pix, pair_lm, pair_count)

    wide = P(("groups", "lat"), "lon", None, "feat")
    flat = P(("groups", "lat"), "lon", "feat")
    return jax.shard_map(
        body,
        mesh=mesh,
        in_specs=(wide, flat, wide, wide, wide, flat, flat, flat),
        out_specs=(wide, wide),
        check_vma=False,
    )
```

time: 382 us -> 37.9 us (0.10)
  waiting for transfers between devices: 257 us -> 0 us
  starting transfers between devices: 68.7 us -> 0 us
  Pallas kernels: 0 us -> 31.8 us
  local copies, waits for them, and re-layouts: 19.5 us -> 4.42 us
  between operations: 14.9 us -> 1.32 us
  matrix products: 10.5 us -> 0 us
  other arithmetic: 4.93 us -> 0 us
    ppermute x8 -> x0, waiting for transfers between devices: 250 us -> none  [the longest x2 217 us: from_behind_2(): lax.ppermute(shard, axis, [(i, (i + by) % devices) for i in range(devices)])]
    ppermute x8 -> x0, starting transfers between devices: 68.6 us -> none  [the longest x2 55.7 us: from_behind_2(): lax.ppermute(shard, axis, [(i, (i + by) % devices) for i in range(devices)])]
    pallas_call x0 -> x1, Pallas kernels: none -> 31.8 us  [body(): pl.pallas_call(functools.partial(kernel, lats, lons), out_shape=(out, out...]
    dot_general x5 -> x0, matrix products: 10.5 us -> none  [the longest x1 4.07 us: kernel_block(): jnp.einsum('gfp,gfl->gpl', pix_rows, lm_rows, precision=lax.Precision.HIG...]
    broadcast_in_dim x4 -> x0, local copies, waits for them, and re-layouts: 9.34 us -> none  [the longest x1 7.87 us: body(): saved_init = jnp.zeros((slot_total, BLOCK, BLOCK), jnp.float32)]
    reduce_scatter x1 -> x0, waiting for transfers between devices: 7.21 us -> none  [body(): owned = lax.psum_scatter(lon_done, 'feat', scatter_dimension=1, tiled=True)]
    gather x6 -> x0, local copies, waits for them, and re-layouts: 5.03 us -> none  [the longest x1 1.59 us: forward_step(): coefficient_tiles[slot_landmark]]
  transfers between devices with their start and end apart: 9 -> 0, of which waited for: 9 -> 0; matrix products, arithmetic and copies ran while one was open for 0% -> 0% of each run, Pallas kernels for 0% -> 0%
where the time goes in v1:
time: 37.9 us; the launch traced here: 37.5 us
  Pallas kernels  31.8 us (84%)
  local copies, waits for them, and re-layouts  4.42 us (12%)
  between operations  1.32 us (3%)
    pallas_call x1, Pallas kernels, body(): pl.pallas_call(functools.partial(kernel, lats, lons), out_shape=(out, out...  31.8 us
    unnamed x14, local copies, waits for them, and re-layouts  3.2 us
    pallas_call x2, local copies, waits for them, and re-layouts, body(): pl.pallas_call(functools.partial(kernel, lats, lons), out_shape=(out, out...  1.23 us

profile of v1, /device:TPU:0, one launch (start us, length us, event | category | flops | bytes accessed | tf_op | source)
XLA Modules:
  0.0 37.5 jit_solution(446471732347414094)
XLA Ops:
  1.3 0.0 copy-start.5
  1.3 0.7 %copy.10.co_ref = f32[1,1,12,256]{3,2,1,0:T(8,128)S(1)} copy(f32[1,1,12,256]{3,1,2,0:T(1,128)} %param.11) | data formatting | bytes 24576 | tf_op args[3]
  2.0 0.0 copy-done.5
  2.0 0.0 copy-start.2
  2.0 0.0 copy-start.3
  2.0 0.0 copy-start.4
  2.0 0.7 %copy-done.2 = s32[1,1,1024]{2,1,0:T(1,128)S(1)} copy-done((s32[1,1,1024]{2,1,0:T(1,128)S(1)}, s32[1,1,1024]{2,1,0:T(1,128)}, u32[]{:S(2)}) %copy-start.2) | copy-done | bytes 4120
  2.7 0.0 copy-done.3
  2.7 0.0 copy-done.4
  2.7 0.0 copy-start
  2.7 0.9 %copy-done = f32[1,1,64,1024]{3,2,1,0:T(8,128)S(1)} copy-done((f32[1,1,64,1024]{3,2,1,0:T(8,128)S(1)}, f32[1,1,64,1024]{3,2,1,0:T(8,128)}, u32[]{:S(2)}) %copy-start) | copy-done | bytes 262168
  3.7 0.0 copy-start.1
  3.7 0.8 %copy-done.1 = f32[1,1,64,256]{3,2,1,0:T(8,128)S(1)} copy-done((f32[1,1,64,256]{3,2,1,0:T(8,128)S(1)}, f32[1,1,64,256]{3,2,1,0:T(8,128)}, u32[]{:S(2)}) %copy-start.1) | copy-done | bytes 65560
  4.5 31.8 %shard_map.95 = (f32[1,1,12,256]{3,2,1,0:T(8,128)S(1)}, f32[1,1,12,256]{3,2,1,0:T(8,128)S(1)}) custom-call(f32[1,1,64,256]{3,2,1,0:T(8,128)S(1)} %copy-done.1, f32[1,1,12,256]{3,2,1,0:T(8,128)S(1)} %copy.10.co_ref, f32[1,1,12,256]{3,2,1,0:T(8,128)S(1)} %copy.11.di_ref, f32[1,1,64,1024]{3,2,1,0:T(8,128)S(1)} %copy-done, s32[1,1,1024]{2,1,0:T(1,128)S(1)} %copy-done.2, ...), custom_call_target="tpu_custom_call" | custom-call | tf_op jit(solution)/shard_map/pallas_call | solution.py:336
  36.3 0.6 %copy.12 = f32[1,1,12,256]{3,1,2,0:T(1,128)} copy(f32[1,1,12,256]{3,2,1,0:T(8,128)S(1)} %get-tuple-element.2) | data formatting | bytes 24576 | tf_op jit(solution)/shard_map/pallas_call | solution.py:336
  36.9 0.6 %copy.13 = f32[1,1,12,256]{3,1,2,0:T(1,128)} copy(f32[1,1,12,256]{3,2,1,0:T(8,128)S(1)} %get-tuple-element.3) | data formatting | bytes 24576 | tf_op jit(solution)/shard_map/pallas_call | solution.py:336
  (1 shorter events, 0.0 us)
Async XLA Ops:
  1.3 0.7 %copy-start.5 = (f32[1,1,12,256]{3,1,2,0:T(1,128)S(1)}, f32[1,1,12,256]{3,1,2,0:T(1,128)}, u32[]{:S(2)}) copy-start(f32[1,1,12,256]{3,1,2,0:T(1,128)} %param.12) | copy-start | bytes 36868
  2.0 0.7 %copy-start.2 = (s32[1,1,1024]{2,1,0:T(1,128)S(1)}, s32[1,1,1024]{2,1,0:T(1,128)}, u32[]{:S(2)}) copy-start(s32[1,1,1024]{2,1,0:T(1,128)} %lab_ref.1) | copy-start | bytes 12292
  2.0 0.7 %copy-start.3 = (s32[1,1,256]{2,1,0:T(1,128)S(1)}, s32[1,1,256]{2,1,0:T(1,128)}, u32[]{:S(2)}) copy-start(s32[1,1,256]{2,1,0:T(1,128)} %pp_ref.1) | copy-start | bytes 3076
  2.0 0.7 %copy-start.4 = (s32[1,1,256]{2,1,0:T(1,128)S(1)}, s32[1,1,256]{2,1,0:T(1,128)}, u32[]{:S(2)}) copy-start(s32[1,1,256]{2,1,0:T(1,128)} %pn_ref.1) | copy-start | bytes 3076
  2.7 0.9 %copy-start = (f32[1,1,64,1024]{3,2,1,0:T(8,128)S(1)}, f32[1,1,64,1024]{3,2,1,0:T(8,128)}, u32[]{:S(2)}) copy-start(f32[1,1,64,1024]{3,2,1,0:T(8,128)} %px_ref.1) | copy-start | bytes 786436
  3.7 0.8 %copy-start.1 = (f32[1,1,64,256]{3,2,1,0:T(8,128)S(1)}, f32[1,1,64,256]{3,2,1,0:T(8,128)}, u32[]{:S(2)}) copy-start(f32[1,1,64,256]{3,2,1,0:T(8,128)} %lm_ref.1) | copy-start | bytes 196612

commit v2 on v1

--- a/solution.py
+++ b/solution.py
@@ -8,7 +8,7 @@
 from jax.sharding import PartitionSpec as P
 
 BLOCK = 128
-CHUNK = 256
+CHUNK = 512
 RADIUS = 5.0
 BF16 = jnp.bfloat16
 F32 = jnp.float32
@@ -41,6 +41,16 @@
 def kernel(
     lats,
     lons,
+    lm_hbm,
+    co_hbm,
+    di_hbm,
+    px_hbm,
+    lab_hbm,
+    pp_hbm,
+    pn_hbm,
+    cnt_ref,
+    grad_ref,
+    hess_ref,
     lm_ref,
     co_ref,
     di_ref,
@@ -48,9 +58,7 @@
     lab_ref,
     pp_ref,
     pn_ref,
-    cnt_ref,
-    grad_ref,
-    hess_ref,
+    load_sem,
     near,
     kern_hi,
     kern_lo,
@@ -59,7 +67,6 @@
     forward,
     back_both,
     back_high,
-    mine,
     part_out,
     part_in,
     tot_out,
@@ -72,12 +79,12 @@
     tot_send,
     tot_recv,
 ):
-    feats, half_lm = lm_ref.shape[2:]
-    classes = co_ref.shape[2]
+    feats, half_lm = lm_ref.shape
+    classes = co_ref.shape[0]
     rows = 2 * classes
-    pix = px_ref.shape[3]
+    pix = px_ref.shape[1]
     depth = pix_rows.shape[1]
-    slots = pp_ref.shape[2]
+    slots = pp_ref.shape[1]
     side = lax.axis_index("feat")
     band = lax.axis_index("lat")
     column = lax.axis_index("lon")
@@ -101,6 +108,23 @@
             else:
                 pl.when(inside(a))(functools.partial(act, a, b))
 
+    loads = [
+        pltpu.make_async_copy(source, target, load_sem.at[n])
+        for n, (source, target) in enumerate(
+            [
+                (lm_hbm.at[0, 0], lm_ref),
+                (co_hbm.at[0], co_ref),
+                (di_hbm.at[0], di_ref),
+                (px_hbm.at[0, 0], px_ref),
+                (pp_hbm.at[0], pp_ref),
+                (pn_hbm.at[0], pn_ref),
+                (lab_hbm.at[0], lab_ref),
+            ]
+        )
+    ]
+    for load in loads:
+        load.start()
+
     barrier = pltpu.get_barrier_semaphore()
 
     def greet(a, b):
@@ -110,9 +134,11 @@
     each_around(greet)
 
     own = 8 + side
-    near[own, 0:feats, :] = lm_ref[0, 0]
-    near[own, feats : feats + classes, :] = co_ref[0, 0]
-    near[own, feats + classes : feats + rows, :] = di_ref[0, 0]
+    for load in loads[:3]:
+        load.wait()
+    near[own, 0:feats, :] = lm_ref[...]
+    near[own, feats : feats + classes, :] = co_ref[:, 0, :]
+    near[own, feats + classes : feats + rows, :] = di_ref[:, 0, :]
 
     bands = sum(inside(a).astype(jnp.int32) for a in (0, 1, 2))
     pl.semaphore_wait(barrier, 3 * bands)
@@ -151,7 +177,9 @@
     pass_copy(4).start()
     each_around(lambda a, b: near_copy(a, b).start())
 
-    pixels = px_ref[0, 0]
+    for load in loads[3:]:
+        load.wait()
+    pixels = px_ref[...]
     x_high, x_low = parts_of(pixels * (-2.0 / (RADIUS * RADIUS)))
     x1, x2, x3 = three_parts(jnp.sum(pixels * pixels, axis=0, keepdims=True) * (1.0 / (RADIUS * RADIUS)))
     row = lax.broadcasted_iota(jnp.int32, (depth - 3 * feats, pix), 0)
@@ -166,10 +194,10 @@
     near_blocks = 18 * half_lm // BLOCK
     used = lax.broadcasted_iota(jnp.int32, (1, slots), 1) < cnt_ref[0, 0, 0]
     pix_hot = jnp.where(
-        jnp.logical_and(lax.broadcasted_iota(jnp.int32, (pix_blocks, slots), 0) == pp_ref[0], used), 1.0, 0.0
+        jnp.logical_and(lax.broadcasted_iota(jnp.int32, (pix_blocks, slots), 0) == pp_ref[...], used), 1.0, 0.0
     ).astype(BF16)
     lm_pad = -(-near_blocks // BLOCK) * BLOCK
-    lm_hot = jnp.where(lax.broadcasted_iota(jnp.int32, (lm_pad, slots), 0) == pn_ref[0], 1.0, 0.0).astype(BF16)
+    lm_hot = jnp.where(lax.broadcasted_iota(jnp.int32, (lm_pad, slots), 0) == pn_ref[...], 1.0, 0.0).astype(BF16)
     counts = dot(pix_hot, lm_hot, NT).astype(BF16)
     width = near_blocks * BLOCK
     spread = jnp.where(
@@ -214,8 +242,10 @@
             value_low = (value - value_high.astype(F32)).astype(BF16)
             kern_hi[place, at, :] = value_high
             kern_lo[place, at, :] = value_low
-            upper = dot(both, value_high, NT)
-            lower = dot(high, value_low, NT)
+        for chunk in range(pix // CHUNK):
+            at = slice(chunk * CHUNK, (chunk + 1) * CHUNK)
+            upper = dot(both, kern_hi[place, at, :], NT)
+            lower = dot(high, kern_lo[place, at, :], NT)
             forward[:, at] += upper[:rows] + upper[rows:] + lower[:rows]
 
     def forward_tile(turn, carry):
@@ -241,7 +271,7 @@
     probe = forward[classes:rows, :]
     powered = jnp.exp(logits - jnp.max(logits, axis=0, keepdims=True))
     chances = powered / jnp.sum(powered, axis=0, keepdims=True)
-    target = jnp.where(lax.broadcasted_iota(jnp.int32, (classes, pix), 0) == lab_ref[0], 1.0, 0.0)
+    target = jnp.where(lax.broadcasted_iota(jnp.int32, (classes, pix), 0) == lab_ref[...], 1.0, 0.0)
     moved = chances * probe
     curv = moved - chances * jnp.sum(moved, axis=0, keepdims=True)
     both, high = stacked_pair(jnp.concatenate([chances - target, curv], axis=0), 32)
@@ -274,7 +304,7 @@
         lower = dot(back_high[...], kern_lo[place], NN)
         return upper[:rows] + upper[rows:] + lower[:rows]
 
-    def backward_tile(turn, carry):
+    def backward_other(turn, carry):
         a, b = order(8 - turn)
         slot = a * 3 + b
 
@@ -282,22 +312,27 @@
         def _():
             part_out[slot] = backward_half(2 * slot + 1 - side)
             part_copy(slot).start()
-            mine[slot] = backward_half(2 * slot + side)
-
-        a_before, b_before = order(9 - turn)
-        before = a_before * 3 + b_before
-
-        @pl.when(jnp.logical_and(turn > 0, inside(a_before)))
+
+        return carry
+
+    def backward_own(turn, carry):
+        a, b = order(8 - turn)
+        slot = a * 3 + b
+
+        @pl.when(inside(a))
         def _():
-            part_copy(before).wait_recv()
-            tot_out[before] = mine[before] + part_in[before]
-            tot_copy(a_before, b_before).start()
+            value = backward_half(2 * slot + side)
+            part_copy(slot).wait_recv()
+            tot_out[slot] = value + part_in[slot]
+
+            @pl.when(turn < 8)
+            def _():
+                tot_copy(a, b).start()
 
         return carry
 
-    lax.fori_loop(0, 9, backward_tile, 0)
-    part_copy(4).wait_recv()
-    tot_out[4] = mine[4] + part_in[4]
+    lax.fori_loop(0, 9, backward_other, 0)
+    lax.fori_loop(0, 9, backward_own, 0)
 
     def take(a, b):
         slot = a * 3 + b
@@ -306,8 +341,8 @@
 
     each_around(take)
     total = tot_out[4]
-    grad_ref[0, 0] = total[:classes]
-    hess_ref[0, 0] = total[classes:]
+    grad_ref[0, :, 0, :] = total[:classes]
+    hess_ref[0, :, 0, :] = total[classes:]
 
     pass_copy(4).wait_send()
     part_copy(4).wait_send()
@@ -330,15 +365,25 @@
         pix = pix_feat.shape[3]
         depth = 4 * feats
         vmem = pl.BlockSpec(memory_space=pltpu.VMEM)
-        out = jax.ShapeDtypeStruct(coefs.shape, F32)
+        classes = coefs.shape[2]
+        out = jax.ShapeDtypeStruct((1, classes, 1, half_lm), F32)
         partial = pltpu.VMEM((9, rows, half_lm), F32)
         nine = pltpu.SemaphoreType.DMA((9,))
-        return pl.pallas_call(
+        flat_class = pltpu.VMEM((classes, 1, half_lm), F32)
+        outs = pl.pallas_call(
             functools.partial(kernel, lats, lons),
             out_shape=(out, out),
-            in_specs=[vmem] * 7 + [pl.BlockSpec(memory_space=pltpu.SMEM)],
+            in_specs=[pl.BlockSpec(memory_space=pltpu.HBM)] * 7 + [pl.BlockSpec(memory_space=pltpu.SMEM)],
             out_specs=(vmem, vmem),
             scratch_shapes=[
+                pltpu.VMEM((feats, half_lm), F32),
+                flat_class,
+                flat_class,
+                pltpu.VMEM((feats, pix), F32),
+                pltpu.VMEM((1, pix), jnp.int32),
+                pltpu.VMEM((1, pair_pix.shape[2]), jnp.int32),
+                pltpu.VMEM((1, pair_pix.shape[2]), jnp.int32),
+                pltpu.SemaphoreType.DMA((7,)),
                 pltpu.VMEM((18, feats + rows, half_lm), F32),
                 pltpu.VMEM((18, pix, half_lm), BF16),
                 pltpu.VMEM((18, pix, half_lm), BF16),
@@ -351,7 +396,6 @@
                 partial,
                 partial,
                 partial,
-                partial,
                 nine,
                 pltpu.SemaphoreType.DMA((18,)),
                 nine,
@@ -361,9 +405,19 @@
                 nine,
             ],
             compiler_params=pltpu.CompilerParams(
-                collective_id=0, has_side_effects=True, vmem_limit_bytes=48 * 1024 * 1024
+                collective_id=0, has_side_effects=True, vmem_limit_bytes=64 * 1024 * 1024 - 65536
             ),
-        )(lm_feat, coefs, direction, pix_feat, labels, pair_pix, pair_lm, pair_count)
+        )(
+            lm_feat,
+            coefs.transpose(0, 2, 1, 3),
+            direction.transpose(0, 2, 1, 3),
+            pix_feat,
+            labels,
+            pair_pix,
+            pair_lm,
+            pair_count,
+        )
+        return tuple(value.transpose(0, 2, 1, 3) for value in outs)
 
     wide = P(("groups", "lat"), "lon", None, "feat")
     flat = P(("groups", "lat"), "lon", "feat")

time: 37.9 us -> 32.7 us (0.86)
  Pallas kernels: 31.8 us -> 29.3 us
  local copies, waits for them, and re-layouts: 4.42 us -> 1.92 us
    pallas_call x1, Pallas kernels: 31.8 us -> 29.3 us  [body(): pl.pallas_call(functools.partial(kernel, lats, lons), out_shape=(out, out...]
    unnamed x14 -> x4, local copies, waits for them, and re-layouts: 3.2 us -> 1.92 us
    pallas_call x2 -> x0, local copies, waits for them, and re-layouts: 1.23 us -> none  [body(): pl.pallas_call(functools.partial(kernel, lats, lons), out_shape=(out, out...]
where the time goes in v2:
time: 32.7 us; the launch traced here: 32.5 us
  Pallas kernels  29.3 us (90%)
  local copies, waits for them, and re-layouts  1.92 us (6%)
  between operations  1.3 us (4%)
    pallas_call x1, Pallas kernels, body(): pl.pallas_call(functools.partial(kernel, lats, lons), out_shape=(out, out...  29.3 us
    unnamed x4, local copies, waits for them, and re-layouts  1.92 us

profile of v2, /device:TPU:0, one launch (start us, length us, event | category | flops | bytes accessed | tf_op | source)
XLA Modules:
  0.0 32.5 jit_solution(4225923582136077136)
XLA Ops:
  1.3 29.3 %shard_map.95 = (f32[1,12,1,256]{3,2,1,0:T(1,128)}, f32[1,12,1,256]{3,2,1,0:T(1,128)}) custom-call(f32[1,1,64,256]{3,2,1,0:T(8,128)} %lm_hbm.1, f32[1,12,1,256]{3,2,1,0:T(1,128)} %bitcast.8, f32[1,12,1,256]{3,2,1,0:T(1,128)} %bitcast.9, f32[1,1,64,1024]{3,2,1,0:T(8,128)} %px_hbm.1, s32[1,1,1024]{2,1,0:T(1,128)} %lab_hbm.1, s32[1,1,256]{2,1,0:T(1,128)} %pp_hbm.1, ...), custom_call_target="tpu_custom_call" | custom-call | tf_op jit(solution)/shard_map/pallas_call | solution.py:373
  30.6 0.0 copy-start
  30.6 1.3 %copy.15 = f32[1,1,12,256]{3,1,2,0:T(1,128)} copy(f32[1,1,12,256]{3,1,2,0:T(1,128)} %bitcast.11) | data formatting | bytes 24576
  31.9 0.0 copy-done
  31.9 0.6 %copy.16 = f32[1,1,12,256]{3,1,2,0:T(1,128)} copy(f32[1,1,12,256]{3,1,2,0:T(1,128)S(1)} %bitcast.10) | data formatting | bytes 24576
Async XLA Ops:
  30.6 1.3 %copy-start = (f32[1,12,1,256]{3,2,1,0:T(1,128)S(1)}, f32[1,12,1,256]{3,2,1,0:T(1,128)}, u32[]{:S(2)}) copy-start(f32[1,12,1,256]{3,2,1,0:T(1,128)} %get-tuple-element.5) | copy-start | bytes 36868

commit v3 on v2

--- a/solution.py
+++ b/solution.py
@@ -97,7 +97,9 @@
         return {"lat": band + a - 1, "lon": lax.rem(column + b - 1 + lons, lons)}
 
     def order(turn):
-        return lax.rem(1 + 2 * lax.rem(turn, 3), 3), lax.rem(1 + 2 * (turn // 3), 3)
+        late = (turn // 3 + 1) // 2
+        a = lax.rem(1 + 2 * ((1 - late) * turn + late * ((turn + 1) // 2 - 2)), 3)
+        return a, 1 - late + late * 2 * lax.rem(turn + 1, 2)
 
     around = [(1, 0), (1, 2), (0, 0), (0, 2), (2, 0), (2, 2), (0, 1), (2, 1)]
 
@@ -144,13 +146,14 @@
     pl.semaphore_wait(barrier, 3 * bands)
 
     def near_copy(a, b):
-        there = (2 - a) * 3 + (2 - b)
+        corner = a != 1 and b != 1
+        there = (2 - a) * 3 + (b if corner else 2 - b)
         return pltpu.make_async_remote_copy(
-            src_ref=near.at[own],
+            src_ref=near.at[2 * (3 + b) + side if corner else own],
             dst_ref=near.at[2 * there + side],
             send_sem=near_send.at[a * 3 + b],
             recv_sem=near_recv.at[2 * there + side],
-            device_id=tile_at(a, b),
+            device_id=tile_at(a, 1 if corner else b),
             device_id_type=pl.DeviceIdType.MESH,
         )
 
@@ -175,7 +178,22 @@
         )
 
     pass_copy(4).start()
-    each_around(lambda a, b: near_copy(a, b).start())
+    def send_own(a, b):
+        if a == 1 or b == 1:
+            near_copy(a, b).start()
+
+    each_around(send_own)
+
+    def send_row():
+        for b in (0, 2):
+            arrived(2 * (3 + b) + side).wait_recv()
+            for a in (0, 2):
+
+                @pl.when(inside(a))
+                def _():
+                    near_copy(a, b).start()
+
+            pass_copy(3 + b).start()
 
     for load in loads[3:]:
         load.wait()
@@ -254,7 +272,11 @@
 
         @pl.when(inside(a))
         def _():
-            @pl.when(turn > 0)
+            @pl.when(turn == 3)
+            def _():
+                send_row()
+
+            @pl.when(jnp.logical_or(turn * (3 - turn) > 0, turn > 4))
             def _():
                 arrived(2 * slot + side).wait_recv()
                 pass_copy(slot).start()

time: 32.7 us -> 30.8 us (0.942)
  Pallas kernels: 29.3 us -> 27.4 us
    pallas_call x1, Pallas kernels: 29.3 us -> 27.4 us  [body(): pl.pallas_call(functools.partial(kernel, lats, lons), out_shape=(out, out...]
where the time goes in v3:
time: 30.8 us; the launch traced here: 30.6 us
  Pallas kernels  27.4 us (89%)
  local copies, waits for them, and re-layouts  1.92 us (6%)
  between operations  1.3 us (4%)
    pallas_call x1, Pallas kernels, body(): pl.pallas_call(functools.partial(kernel, lats, lons), out_shape=(out, out...  27.4 us
    unnamed x4, local copies, waits for them, and re-layouts  1.92 us

profile of v3, /device:TPU:0, one launch (start us, length us, event | category | flops | bytes accessed | tf_op | source)
XLA Modules:
  0.0 30.6 jit_solution(1013085715789717863)
XLA Ops:
  1.3 27.4 %shard_map.95 = (f32[1,12,1,256]{3,2,1,0:T(1,128)}, f32[1,12,1,256]{3,2,1,0:T(1,128)}) custom-call(f32[1,1,64,256]{3,2,1,0:T(8,128)} %lm_hbm.1, f32[1,12,1,256]{3,2,1,0:T(1,128)} %bitcast.8, f32[1,12,1,256]{3,2,1,0:T(1,128)} %bitcast.9, f32[1,1,64,1024]{3,2,1,0:T(8,128)} %px_hbm.1, s32[1,1,1024]{2,1,0:T(1,128)} %lab_hbm.1, s32[1,1,256]{2,1,0:T(1,128)} %pp_hbm.1, ...), custom_call_target="tpu_custom_call" | custom-call | tf_op jit(solution)/shard_map/pallas_call | solution.py:395
  28.7 0.0 copy-start
  28.7 1.3 %copy.15 = f32[1,1,12,256]{3,1,2,0:T(1,128)} copy(f32[1,1,12,256]{3,1,2,0:T(1,128)} %bitcast.11) | data formatting | bytes 24576
  30.0 0.0 copy-done
  30.0 0.6 %copy.16 = f32[1,1,12,256]{3,1,2,0:T(1,128)} copy(f32[1,1,12,256]{3,1,2,0:T(1,128)S(1)} %bitcast.10) | data formatting | bytes 24576
Async XLA Ops:
  28.7 1.3 %copy-start = (f32[1,12,1,256]{3,2,1,0:T(1,128)S(1)}, f32[1,12,1,256]{3,2,1,0:T(1,128)}, u32[]{:S(2)}) copy-start(f32[1,12,1,256]{3,2,1,0:T(1,128)} %get-tuple-element.5) | copy-start | bytes 36868

commit v4 on v3

--- a/solution.py
+++ b/solution.py
@@ -96,10 +96,12 @@
     def tile_at(a, b):
         return {"lat": band + a - 1, "lon": lax.rem(column + b - 1 + lons, lons)}
 
+    first = 2 * (column == 0).astype(jnp.int32)
+
     def order(turn):
         late = (turn // 3 + 1) // 2
         a = lax.rem(1 + 2 * ((1 - late) * turn + late * ((turn + 1) // 2 - 2)), 3)
-        return a, 1 - late + late * 2 * lax.rem(turn + 1, 2)
+        return a, 1 - late + late * (first + (1 - first) * 2 * lax.rem(turn + 1, 2))
 
     around = [(1, 0), (1, 2), (0, 0), (0, 2), (2, 0), (2, 2), (0, 1), (2, 1)]
 
@@ -145,8 +147,7 @@
     bands = sum(inside(a).astype(jnp.int32) for a in (0, 1, 2))
     pl.semaphore_wait(barrier, 3 * bands)
 
-    def near_copy(a, b):
-        corner = a != 1 and b != 1
+    def near_copy(a, b, corner):
         there = (2 - a) * 3 + (b if corner else 2 - b)
         return pltpu.make_async_remote_copy(
             src_ref=near.at[2 * (3 + b) + side if corner else own],
@@ -180,20 +181,19 @@
     pass_copy(4).start()
     def send_own(a, b):
         if a == 1 or b == 1:
-            near_copy(a, b).start()
+            near_copy(a, b, False).start()
 
     each_around(send_own)
 
-    def send_row():
-        for b in (0, 2):
-            arrived(2 * (3 + b) + side).wait_recv()
-            for a in (0, 2):
-
-                @pl.when(inside(a))
-                def _():
-                    near_copy(a, b).start()
-
-            pass_copy(3 + b).start()
+    def relay(b):
+        arrived(2 * (3 + b) + side).wait_recv()
+        for a in (0, 2):
+
+            @pl.when(inside(a))
+            def _():
+                near_copy(a, b, True).start()
+
+        pass_copy(3 + b).start()
 
     for load in loads[3:]:
         load.wait()
@@ -274,7 +274,7 @@
         def _():
             @pl.when(turn == 3)
             def _():
-                send_row()
+                relay(first)
 
             @pl.when(jnp.logical_or(turn * (3 - turn) > 0, turn > 4))
             def _():
@@ -282,6 +282,11 @@
                 pass_copy(slot).start()
 
             forward_half(2 * slot + side)
+
+            @pl.when(turn == 3)
+            def _():
+                relay(2 - first)
+
             arrived(2 * slot + 1 - side).wait_recv()
             forward_half(2 * slot + 1 - side)
 
@@ -370,7 +375,7 @@
     part_copy(4).wait_send()
 
     def drain(a, b):
-        near_copy(a, b).wait_send()
+        near_copy(a, b, a != 1 and b != 1).wait_send()
         pass_copy(a * 3 + b).wait_send()
         part_copy(a * 3 + b).wait_send()
         tot_copy(a, b).wait_send()

time: 30.8 us -> 30.7 us (level)
  no operation moved by 1% of the time
where the time goes in v4:
time: 30.7 us; the launch traced here: 30.5 us
  Pallas kernels  27.3 us (89%)
  local copies, waits for them, and re-layouts  1.92 us (6%)
  between operations  1.3 us (4%)
    pallas_call x1, Pallas kernels, body(): pl.pallas_call(functools.partial(kernel, lats, lons), out_shape=(out, out...  27.3 us
    unnamed x4, local copies, waits for them, and re-layouts  1.92 us

profile of v4, /device:TPU:0, one launch (start us, length us, event | category | flops | bytes accessed | tf_op | source)
XLA Modules:
  0.0 30.5 jit_solution(12503508226709076185)
XLA Ops:
  1.3 27.3 %shard_map.95 = (f32[1,12,1,256]{3,2,1,0:T(1,128)}, f32[1,12,1,256]{3,2,1,0:T(1,128)}) custom-call(f32[1,1,64,256]{3,2,1,0:T(8,128)} %lm_hbm.1, f32[1,12,1,256]{3,2,1,0:T(1,128)} %bitcast.8, f32[1,12,1,256]{3,2,1,0:T(1,128)} %bitcast.9, f32[1,1,64,1024]{3,2,1,0:T(8,128)} %px_hbm.1, s32[1,1,1024]{2,1,0:T(1,128)} %lab_hbm.1, s32[1,1,256]{2,1,0:T(1,128)} %pp_hbm.1, ...), custom_call_target="tpu_custom_call" | custom-call | tf_op jit(solution)/shard_map/pallas_call | solution.py:400
  28.6 0.0 copy-start
  28.6 1.3 %copy.15 = f32[1,1,12,256]{3,1,2,0:T(1,128)} copy(f32[1,1,12,256]{3,1,2,0:T(1,128)} %bitcast.11) | data formatting | bytes 24576
  29.9 0.0 copy-done
  29.9 0.6 %copy.16 = f32[1,1,12,256]{3,1,2,0:T(1,128)} copy(f32[1,1,12,256]{3,1,2,0:T(1,128)S(1)} %bitcast.10) | data formatting | bytes 24576
Async XLA Ops:
  28.6 1.3 %copy-start = (f32[1,12,1,256]{3,2,1,0:T(1,128)S(1)}, f32[1,12,1,256]{3,2,1,0:T(1,128)}, u32[]{:S(2)}) copy-start(f32[1,12,1,256]{3,2,1,0:T(1,128)} %get-tuple-element.5) | copy-start | bytes 36868
